TPU v7x, 256 devices: a whole 4x4x8 slice. The times are simulated.
256 devices in a mesh: grp: 8 (over y, core), row: 32 (over x, z).
Axes of the slice: x: 4, y: 4, z: 8, core: 2. Of those that a mesh axis runs over, the one named last changes fastest.
Arguments:
- labeled: bfloat16 [4, 1024, 1024], P(None, 'row', 'grp'), may hold values from -6 to 6
- candidates: bfloat16 [8192, 1024], P(('grp', 'row')), may hold values from -6 to 6
- factor_rows: bfloat16 [4, 1024, 4096], P(None, 'row'), may hold values from -6 to 6
- block_inverse: bfloat16 [4, 1024, 1024], P(None, 'row'), as said below
Outputs:
- whitened: bfloat16 [4, 1024, 8192], P(None, 'row', 'grp')
- explained: float32 [8192], P('grp')
Inputs may be any that keep to these rules, and one draw needn't show every extreme that they name: Each block of block_inverse is lower triangular with a positive diagonal; it is given as is and is not derived from factor_rows.
All inputs are finite; a program needn't handle non-finite values.
Results may differ from a plain program's by a relative error of at most 0.0075.
Values may be sent and summed in bfloat16 or wider, within the bound.
A program may use at most 64 MiB of HBM per device.

v0:
```python
import math

import jax
import jax.numpy as jnp
from jax import lax
from jax.sharding import PartitionSpec as P


def on_device(labeled, candidates, factor_rows, block_inverse):
    gathered = lax.all_gather(labeled, "grp", axis=2, tiled=True)
    block_count = gathered.shape[0]
    own_count = gathered.shape[1]
    feature_width = gathered.shape[2]
    block_size = block_inverse.shape[2]
    kernel_scale = 0.5 / math.sqrt(feature_width)
    flat_rows = gathered.reshape(block_count * own_count, feature_width)
    kernel = jnp.exp(
        jnp.dot(
            flat_rows,
            lax.all_gather(candidates, "row", axis=0, tiled=True).T,
            preferred_element_type=jnp.float32,
        )
        * kernel_scale
    )
    cand_count = kernel.shape[1]
    kernel = kernel.reshape(block_count, own_count, cand_count)
    pending = [kernel[number] for number in range(block_count)]
    position = lax.axis_index("row")
    solved_own = []
    for number in range(block_count):
        rounded = pending[number].astype(jnp.bfloat16)
        residual_block = lax.all_gather(rounded, "row", axis=0, tiled=True)
        solved = jnp.dot(
            lax.all_gather(block_inverse[number], "row", axis=0, tiled=True),
            residual_block,
            preferred_element_type=jnp.float32,
        ).astype(jnp.bfloat16)
        own_rows = lax.dynamic_slice_in_dim(solved, position * own_count, own_count, 0)
        solved_own.append(own_rows)
        lower_edge = number * block_size
        upper_edge = (number + 1) * block_size
        if number + 1 < block_count:
            panel = factor_rows[number + 1 :, :, lower_edge:upper_edge]
            later_count = block_count - number - 1
            updates = jnp.dot(
                panel.reshape(later_count * own_count, block_size),
                solved,
                preferred_element_type=jnp.float32,
            )
            updates = updates.reshape(later_count, own_count, cand_count)
            for later in range(later_count):
                pending[number + 1 + later] = pending[number + 1 + later] - updates[later]
    whitened = jnp.stack(solved_own, axis=0)
    squares = jnp.sum(jnp.square(whitened.astype(jnp.float32)), axis=(0, 1))
    explained = lax.psum(squares, "row")
    return (whitened, explained)


def solution(mesh):
    in_specs = (
        P(None, "row", "grp"),
        P(("grp", "row"), None),
        P(None, "row", None),
        P(None, "row", None),
    )
    out_specs = (P(None, "row", "grp"), P("grp"))
    return jax.shard_map(
        on_device, mesh=mesh, in_specs=in_specs, out_specs=out_specs, check_vma=False
    )
```

profile of v0, /device:TPU:8, one launch (start us, length us, event | category | flops | bytes accessed | tf_op | source)
XLA Modules:
  0.0 799.7 jit_solution(2571886401627066954)
XLA Ops:
  7.2 0.0 all-gather.14.cloned.1.call-start
  7.2 0.7 all-gather.14.cloned.1.call-update
  7.9 0.0 all-gather.24.cloned.1.call-start
  7.9 1.7 fusion.25
  9.6 0.0 all-gather.24.cloned.1.call-update
  9.6 0.0 all-gather.16.cloned.1.call-start
  9.7 12.3 %all_gather.30 = bf16[4,32,1024]{2,1,0:T(8,128)(2,1)S(1)} all-gather(bf16[4,32,128]{2,1,0:T(8,128)(2,1)} %param.4), channel_id=1, replica_groups=mesh['grp'=8,'row'=32] {'grp'}, dimensions={2}, use_global_device_ids=true | all-gather | bytes 294912 | tf_op jit(solution)/shard_map/all_gather | solution.py:10
  22.0 69.4 %all-gather.14.cloned.1.call-done = bf16[1024,1024]{1,0:T(8,128)(2,1)} async-done(((bf16[32,1024]{1,0:T(8,128)(2,1)}), bf16[1024,1024]{1,0:T(8,128)(2,1)}) %all-gather.14.cloned.1.call-update) | async-done | bytes 2097168 | tf_op jit(solution)/shard_map/all_gather | solution.py:20
  91.4 2.4 fusion.17
  93.8 0.6 slice.106
  94.4 0.0 all-gather.16.cloned.1.call-update
  94.5 0.0 all-gather.26.cloned.1.call-start
  94.5 0.5 all-gather.26.cloned.1.call-update
  95.0 0.0 all-gather.18.cloned.1.call-start
  95.1 0.9 slice.61
  96.0 73.1 %all-gather.24.cloned.1.call-done = bf16[1,1024,1024]{2,1,0:T(8,128)(2,1)} async-done(((bf16[1,32,1024]{2,1,0:T(8,128)(2,1)}), bf16[1,1024,1024]{2,1,0:T(8,128)(2,1)}) %all-gather.24.cloned.1.call-update) | async-done | bytes 2097168 | tf_op jit(solution)/shard_map/all_gather | solution.py:34
  169.1 78.3 %all-gather.16.cloned.1.call-done = bf16[1024,1024]{1,0:T(8,128)(2,1)} async-done(((bf16[32,1024]{1,0:T(8,128)(2,1)}), bf16[1024,1024]{1,0:T(8,128)(2,1)}) %all-gather.16.cloned.1.call-update) | async-done | bytes 2097168 | tf_op jit(solution)/shard_map/all_gather | solution.py:32
  247.4 4.5 fusion.8
  252.0 0.0 copy-start.1
  252.0 1.3 copy-done.1
  253.3 0.5 convolution_bitcast_fusion
  253.8 0.7 fusion.21
  254.5 0.0 all-gather.18.cloned.1.call-update
  254.5 0.0 all-gather.28.cloned.1.call-start
  254.5 0.5 all-gather.28.cloned.1.call-update
  255.1 0.0 all-gather.20.cloned.1.call-start
  255.1 0.9 slice.66
  256.0 69.0 %all-gather.26.cloned.1.call-done = bf16[1,1024,1024]{2,1,0:T(8,128)(2,1)} async-done(((bf16[1,32,1024]{2,1,0:T(8,128)(2,1)}), bf16[1,1024,1024]{2,1,0:T(8,128)(2,1)}) %all-gather.26.cloned.1.call-update) | async-done | bytes 2097168 | tf_op jit(solution)/shard_map/all_gather | solution.py:34
  325.0 78.2 %all-gather.18.cloned.1.call-done = bf16[1024,1024]{1,0:T(8,128)(2,1)} async-done(((bf16[32,1024]{1,0:T(8,128)(2,1)}), bf16[1024,1024]{1,0:T(8,128)(2,1)}) %all-gather.18.cloned.1.call-update) | async-done | bytes 2097168 | tf_op jit(solution)/shard_map/all_gather | solution.py:32
  403.2 4.5 fusion.11
  407.8 0.0 copy-start
  407.8 1.4 copy-done
  409.1 0.5 convolution_bitcast_fusion.1
  409.6 0.7 fusion.20
  410.3 0.0 all-gather.20.cloned.1.call-update
  410.3 0.0 all-gather.30.cloned.1.call-start
  410.4 0.7 all-gather.30.cloned.1.call-update
  411.1 0.0 all-gather.22.cloned.1.call-start
  411.1 69.7 %all-gather.28.cloned.1.call-done = bf16[1,1024,1024]{2,1,0:T(8,128)(2,1)} async-done(((bf16[1,32,1024]{2,1,0:T(8,128)(2,1)}), bf16[1,1024,1024]{2,1,0:T(8,128)(2,1)}) %all-gather.28.cloned.1.call-update) | async-done | bytes 2097168 | tf_op jit(solution)/shard_map/all_gather | solution.py:34
  480.8 78.3 %all-gather.20.cloned.1.call-done = bf16[1024,1024]{1,0:T(8,128)(2,1)} async-done(((bf16[32,1024]{1,0:T(8,128)(2,1)}), bf16[1024,1024]{1,0:T(8,128)(2,1)}) %all-gather.20.cloned.1.call-update) | async-done | bytes 2097168 | tf_op jit(solution)/shard_map/all_gather | solution.py:32
  559.1 4.5 fusion.14
  563.7 1.9 fusion.19
  565.6 0.0 all-gather.22.cloned.1.call-update
  565.6 0.8 dynamic-slice_bitcast_fusion.2
  566.5 0.8 dynamic-slice_bitcast_fusion.1
  567.3 69.5 %all-gather.30.cloned.1.call-done = bf16[1,1024,1024]{2,1,0:T(8,128)(2,1)} async-done(((bf16[1,32,1024]{2,1,0:T(8,128)(2,1)}), bf16[1,1024,1024]{2,1,0:T(8,128)(2,1)}) %all-gather.30.cloned.1.call-update) | async-done | bytes 2097168 | tf_op jit(solution)/shard_map/all_gather | solution.py:34
  636.9 78.3 %all-gather.22.cloned.1.call-done = bf16[1024,1024]{1,0:T(8,128)(2,1)} async-done(((bf16[32,1024]{1,0:T(8,128)(2,1)}), bf16[1024,1024]{1,0:T(8,128)(2,1)}) %all-gather.22.cloned.1.call-update) | async-done | bytes 2097168 | tf_op jit(solution)/shard_map/all_gather | solution.py:32
  715.2 4.5 fusion
  719.8 0.7 multiply_reduce_fusion
  720.5 72.7 %psum.7 = f32[1024]{0:T(1024)} all-reduce(f32[1024]{0:T(1024)S(1)} %get-tuple-element.2), channel_id=1, replica_groups=mesh['grp'=8,'row'=32] {'row'}, use_global_device_ids=true, to_apply=%region_1.0 | all-reduce | flops 1024 | bytes 8192 | tf_op jit(solution)/shard_map/psum | solution.py:55
  (2 shorter events, 0.0 us)
Async XLA Ops:
  7.2 84.2 %all-gather.14.cloned.1.call-start = ((), (), s32[]{:S(2)}) async-start(), calls=%async_computation | async-start | bytes 2162688 | tf_op jit(solution)/shard_map/all_gather | solution.py:20
  7.9 161.2 %all-gather.24.cloned.1.call-start = ((), (), s32[]{:S(2)}) async-start(), calls=%async_computation.5 | async-start | bytes 2162688 | tf_op jit(solution)/shard_map/all_gather | solution.py:34
  9.6 237.8 %all-gather.16.cloned.1.call-start = ((), (), s32[]{:S(2)}) async-start(), calls=%async_computation.1 | async-start | bytes 2162688 | tf_op jit(solution)/shard_map/all_gather | solution.py:32
  94.5 230.6 %all-gather.26.cloned.1.call-start = ((), (), s32[]{:S(2)}) async-start(), calls=%async_computation.6 | async-start | bytes 2162688 | tf_op jit(solution)/shard_map/all_gather | solution.py:34
  95.0 308.1 %all-gather.18.cloned.1.call-start = ((), (), s32[]{:S(2)}) async-start(), calls=%async_computation.2 | async-start | bytes 2162688 | tf_op jit(solution)/shard_map/all_gather | solution.py:32
  252.0 1.3 copy-start.1
  254.5 226.3 %all-gather.28.cloned.1.call-start = ((), (), s32[]{:S(2)}) async-start(), calls=%async_computation.7 | async-start | bytes 2162688 | tf_op jit(solution)/shard_map/all_gather | solution.py:34
  255.1 304.1 %all-gather.20.cloned.1.call-start = ((), (), s32[]{:S(2)}) async-start(), calls=%async_computation.3 | async-start | bytes 2162688 | tf_op jit(solution)/shard_map/all_gather | solution.py:32
  407.8 1.4 copy-start
  410.3 226.5 %all-gather.30.cloned.1.call-start = ((), (), s32[]{:S(2)}) async-start(), calls=%async_computation.8 | async-start | bytes 2162688 | tf_op jit(solution)/shard_map/all_gather | solution.py:34
  411.1 304.1 %all-gather.22.cloned.1.call-start = ((), (), s32[]{:S(2)}) async-start(), calls=%async_computation.4 | async-start | bytes 2162688 | tf_op jit(solution)/shard_map/all_gather | solution.py:32
Sparse Core Ops, SparseCore 0:
  10.6 80.7 all-gather.13
  94.0 75.1 all-gather.23
  172.3 75.1 all-gather.15
  249.9 75.1 all-gather.25
  328.0 75.1 all-gather.17
  405.6 75.1 all-gather.27
  484.0 75.1 all-gather.19
  561.7 75.1 all-gather.29
  640.0 75.1 all-gather.21
where the time goes:
time: 800 us
  waiting for transfers between devices  666 us (83%)
  blocking collectives  85 us (11%)
  matrix products  23.5 us (3%)
  between operations  13.9 us (2%)
  local copies, waits for them, and re-layouts  8.57 us (1%)
    all_gather x4, waiting for transfers between devices, on_device(): residual_block = lax.all_gather(rounded, 'row', axis=0, tiled=True)  313 us
    all_gather x4, waiting for transfers between devices, on_device(): lax.all_gather(block_inverse[number], 'row', axis=0, tiled=True)  281 us
    psum x1, blocking collectives, on_device(): explained = lax.psum(squares, 'row')  72.7 us
    all_gather x1, waiting for transfers between devices, on_device(): lax.all_gather(candidates, 'row', axis=0, tiled=True)  69.4 us
    dot_general x4, matrix products, on_device(): jnp.dot(lax.all_gather(block_inverse[number], 'row', axis=0, tiled=True),...  18.2 us
  transfers between devices with their start and end apart: 9, of which 9 were waited for; matrix products, arithmetic and copies ran while one was open for 3% of the time, Pallas kernels for 0%

commit v1 on v0

v1 whole, which is shorter than its diff:
```python
import functools
import math

import jax
import jax.numpy as jnp
from jax import lax
from jax.experimental import pallas as pl
from jax.experimental.pallas import tpu as pltpu
from jax.sharding import PartitionSpec as P

MESH = pl.DeviceIdType.MESH
BF = jnp.bfloat16
NX, NY, NZ = 4, 4, 8
QUARTER = 256
COLS = 128


def dot(a, b):
    return jnp.dot(a, b, preferred_element_type=jnp.float32)


def kernel(
    scale,
    lab,
    cand,
    fac,
    inv,
    out,
    expl,
    lbuf,
    cbuf,
    ibuf,
    fbuf0,
    fbuf1,
    fbuf2,
    kbuf,
    rbuf,
    wbuf,
    obuf,
    epart,
    esum,
    l1s,
    l1r,
    l2s,
    l2r,
    l3s,
    l3r,
    cs,
    cr,
    i1s,
    i1r,
    i2s,
    i2r,
    i3s,
    i3r,
    f1s,
    f1r,
    f2s,
    f2r,
    f3s,
    f3r,
    rs,
    rr,
    os,
    orr,
    es,
    er,
):
    g = lax.axis_index("grp")
    r = lax.axis_index("row")
    y, c = g // 2, g % 2
    x, z = r // NZ, r % NZ
    fbufs = (fbuf0, fbuf1, fbuf2)
    groups = ((0, 1), (1, 4))

    def x_peer(d):
        return (g, ((x + d) % NX) * NZ + z)

    def y_peer(d):
        return (((y + d) % NY) * 2 + c, r)

    def z_peer(d):
        return (g, x * NZ + (z + d) % NZ)

    core_peer = (y * 2 + 1 - c, r)

    def send(src, dst, ssem, rsem, device):
        pltpu.make_async_remote_copy(
            src_ref=src,
            dst_ref=dst,
            send_sem=ssem,
            recv_sem=rsem,
            device_id=device,
            device_id_type=MESH,
        ).start()

    def local(src, dst, sem):
        pltpu.make_async_copy(src, dst, sem).start()

    def await_bytes(ref, sem):
        pltpu.make_async_copy(ref, ref, sem).wait()

    def each_z(body):
        def step(d, carry):
            body(z_peer(d))
            return carry

        lax.fori_loop(1, NZ, step, 0)

    def rows_of(position):
        return pl.ds(pl.multiple_of(position * 32, 32), 32)

    own_rows = rows_of(z)

    def lab_z(k):
        lo, hi = groups[k]
        dst = lbuf.at[c, y, lo:hi, own_rows, :]
        local(lab.at[lo:hi], dst, l1r.at[k])
        each_z(lambda peer: send(lab.at[lo:hi], dst, l1s.at[k], l1r.at[k], peer))

    def lab_y(k):
        lo, hi = groups[k]
        await_bytes(lbuf.at[c, y, lo:hi], l1r.at[k])
        for d in range(1, NY):
            block = lbuf.at[c, y, lo:hi]
            send(block, block, l2s.at[k], l2r.at[k], y_peer(d))

    def lab_core(k):
        lo, hi = groups[k]
        await_bytes(lbuf.at[c, 0:3, lo:hi], l2r.at[k])
        block = lbuf.at[c, :, lo:hi]
        send(block, block, l3s.at[k], l3r.at[k], core_peer)

    def lab_wait(k):
        lo, hi = groups[k]
        await_bytes(lbuf.at[1 - c, :, lo:hi], l3r.at[k])

    def by_x(body):
        for number in range(NX):
            pl.when(x == number)(functools.partial(body, number))

    def inv_part(b, number, core):
        return ibuf.at[b, number, :, core, :, : (number + 1) * QUARTER]

    def inv_z(b):
        def go(number):
            width = (number + 1) * QUARTER
            src = inv.at[b, pl.ds(pl.multiple_of(c * 16, 16), 16), :width]
            dst = ibuf.at[b, number, z, c, :, :width]
            local(src, dst, i1r.at[b])
            each_z(lambda peer: send(src, dst, i1s.at[b], i1r.at[b], peer))

        by_x(go)

    def inv_x(b):
        def go(number):
            part = inv_part(b, number, c)
            await_bytes(part, i1r.at[b])
            if b < 3:
                for d in range(1, NX):
                    send(part, part, i2s.at[b], i2r.at[b, number], x_peer(d))
            send(part, part, i3s.at[b], i3r.at[b, number], core_peer)

        by_x(go)

    def inv_core(b):
        for number in range(NX):

            @pl.when(x != number)
            def _():
                part = inv_part(b, number, c)
                await_bytes(part, i2r.at[b, number])
                send(part, part, i3s.at[b], i3r.at[b, number], core_peer)

    def inv_wait(b):
        if b < 3:
            for number in range(NX):
                await_bytes(inv_part(b, number, 1 - c), i3r.at[b, number])
        else:
            by_x(lambda number: await_bytes(inv_part(b, number, 1 - c), i3r.at[b, number]))

    def fac_z(j):
        src = fac.at[j + 1 : 4, :, pl.ds(pl.multiple_of(j * 1024 + g * 128, 128), 128)]
        dst = fbufs[j].at[c, y, :, own_rows, :]
        local(src, dst, f1r.at[j])
        each_z(lambda peer: send(src, dst, f1s.at[j], f1r.at[j], peer))

    def fac_y(j):
        block = fbufs[j].at[c, y]
        await_bytes(block, f1r.at[j])
        for d in range(1, NY):
            send(block, block, f2s.at[j], f2r.at[j], y_peer(d))

    def fac_core(j):
        await_bytes(fbufs[j].at[c, 0:3], f2r.at[j])
        half = fbufs[j].at[c]
        send(half, half, f3s.at[j], f3r.at[j], core_peer)

    def fac_wait(j):
        await_bytes(fbufs[j].at[1 - c], f3r.at[j])

    def make_kernel(b):
        rows = jnp.concatenate([lbuf[k % 2, k // 2, b] for k in range(8)], axis=1)
        sums = lax.dot_general(
            rows,
            cbuf[...].reshape(COLS, 1024),
            (((1,), (1,)), ((), ())),
            preferred_element_type=jnp.float32,
        )
        kbuf[b] = jnp.exp(sums * scale)

    def publish(b):
        rbuf[b, x] = kbuf[b].astype(BF)
        for d in range(1, NX):
            send(rbuf.at[b, x], rbuf.at[b, x], rs.at[b], rr.at[b], x_peer(d))

    def residual_wait(b):
        await_bytes(rbuf.at[b, 0:3], rr.at[b])

    def solve(b):
        residual = rbuf[b].reshape(1024, COLS)

        def rows(number):
            width = (number + 1) * QUARTER
            left = ibuf[b, number, :, :, :, :width].reshape(QUARTER, width)
            wbuf[b, number] = dot(left, residual[:width]).astype(BF)

        if b < 3:
            for number in range(NX):
                rows(number)
        else:
            by_x(rows)

    def spread(b):
        dst = obuf.at[z, b]
        local(wbuf.at[b, x, own_rows, :], dst, orr.at[b])

        def step(d, carry):
            other = (z + d) % NZ
            send(
                wbuf.at[b, x, rows_of(other), :],
                dst,
                os.at[b],
                orr.at[b],
                (g, x * NZ + other),
            )
            return carry

        lax.fori_loop(1, NZ, step, 0)

    def update(j, b):
        panel = jnp.concatenate(
            [fbufs[j][k % 2, k // 2, b - j - 1] for k in range(8)], axis=1
        )
        kbuf[b] = kbuf[b] - dot(panel, wbuf[j].reshape(1024, COLS))

    barrier = pltpu.get_barrier_semaphore()
    peers = [x_peer(d) for d in range(1, NX)] + [y_peer(d) for d in range(1, NY)]
    peers += [z_peer(d) for d in range(1, NZ)] + [core_peer]
    for peer in peers:
        pl.semaphore_signal(barrier, inc=1, device_id=peer, device_id_type=MESH)
    pl.semaphore_wait(barrier, len(peers))

    lab_z(0)
    local(cand, cbuf.at[x], cr)
    for d in range(1, NX):
        send(cand, cbuf.at[x], cs, cr, x_peer(d))
    inv_z(0)
    lab_z(1)
    fac_z(0)
    lab_y(0)
    inv_z(1)
    inv_x(0)
    fac_z(1)
    inv_z(2)
    fac_z(2)
    inv_z(3)
    lab_core(0)
    lab_y(1)
    await_bytes(cbuf, cr)
    lab_wait(0)
    make_kernel(0)
    publish(0)
    fac_y(0)
    inv_core(0)
    inv_x(1)
    lab_core(1)
    inv_wait(0)
    residual_wait(0)
    solve(0)
    spread(0)
    fac_core(0)
    lab_wait(1)
    for b in range(1, 4):
        make_kernel(b)
    fac_wait(0)
    update(0, 1)
    publish(1)
    inv_core(1)
    fac_y(1)
    inv_x(2)
    update(0, 2)
    update(0, 3)
    inv_wait(1)
    residual_wait(1)
    solve(1)
    spread(1)
    fac_core(1)
    fac_wait(1)
    update(1, 2)
    publish(2)
    inv_core(2)
    fac_y(2)
    inv_x(3)
    update(1, 3)
    inv_wait(2)
    residual_wait(2)
    solve(2)
    spread(2)
    fac_core(2)
    fac_wait(2)
    update(2, 3)
    publish(3)

    for k, (lo, hi) in enumerate(groups):
        await_bytes(lbuf.at[c, y, lo:hi, 0:224, :], l1s.at[k])
        await_bytes(lbuf.at[c, 0:3, lo:hi], l2s.at[k])
        await_bytes(lbuf.at[c, :, lo:hi], l3s.at[k])
    await_bytes(cbuf.at[0:3], cs)
    for j in range(3):
        await_bytes(fbufs[j].at[c, y, :, 0:224, :], f1s.at[j])
        await_bytes(fbufs[j].at[c, 0:3], f2s.at[j])
        await_bytes(fbufs[j].at[c], f3s.at[j])

    def owed(number):
        for b in range(4):
            part = inv_part(b, number, c)
            await_bytes(ibuf.at[b, number, 0:7, c, :, : (number + 1) * QUARTER], i1s.at[b])
            if b < 3:
                for _ in range(1, NX):
                    await_bytes(part, i2s.at[b])

    by_x(owed)
    for b in range(3):
        for number in range(NX):
            await_bytes(inv_part(b, number, c), i3s.at[b])
    by_x(lambda number: await_bytes(inv_part(3, number, c), i3s.at[3]))
    inv_wait(3)
    residual_wait(3)
    solve(3)
    spread(3)

    total = jnp.zeros((1, COLS), jnp.float32)
    for b in range(4):
        values = wbuf[b, x].astype(jnp.float32)
        total = total + jnp.sum(values * values, axis=0, keepdims=True)
    epart[x] = total
    for d in range(1, NX):
        send(epart.at[x], epart.at[x], es.at[0], er.at[0], x_peer(d))
    await_bytes(epart.at[0:3], er.at[0])
    esum[z] = epart[0] + epart[1] + epart[2] + epart[3]
    each_z(lambda peer: send(esum.at[z], esum.at[z], es.at[1], er.at[1], peer))

    source = lax.broadcasted_iota(jnp.int32, (512, 128), 0)
    target = lax.broadcasted_iota(jnp.int32, (512, 128), 1)
    pickers = []
    for chunk in range(NX):
        wanted = (target // 32) * 128 + chunk * 32 + target % 32
        pickers.append(jnp.where(source == wanted, 1.0, 0.0).astype(BF))
    for b in range(4):
        await_bytes(obuf.at[:, b], orr.at[b])
    for half in range(2):
        rows = jnp.concatenate(
            [obuf[half * 4 + k].reshape(128, COLS) for k in range(4)], axis=1
        )
        for chunk in range(NX):
            tile = dot(rows, pickers[chunk]).astype(BF)
            tile = tile.reshape(4, 32, COLS)
            at = (chunk * 2 + half) * 128
            for b in range(4):
                out[b, :, at : at + 128] = tile[b]

    await_bytes(esum.at[0:7], er.at[1])
    lane = lax.broadcasted_iota(jnp.int32, (1, 128), 1) // 32
    for chunk in range(NX):
        for half in range(2):
            row = jnp.zeros((1, COLS), jnp.float32)
            for k in range(4):
                moved = pltpu.roll(esum[half * 4 + k], ((k - chunk) % 4) * 32, 1)
                row = jnp.where(lane == k, moved, row)
            expl[chunk * 2 + half : chunk * 2 + half + 1, :] = row

    for b in range(4):
        await_bytes(rbuf.at[b, 0:3], rs.at[b])
        await_bytes(obuf.at[0:7, b], os.at[b])
    await_bytes(epart.at[0:3], es.at[0])
    await_bytes(esum.at[0:7], es.at[1])


def on_device(labeled, candidates, factor_rows, block_inverse):
    dma = pltpu.SemaphoreType.DMA
    scale = 0.5 / math.sqrt(1024)
    whitened, explained = pl.pallas_call(
        functools.partial(kernel, scale),
        out_shape=(
            jax.ShapeDtypeStruct((4, 32, 1024), BF),
            jax.ShapeDtypeStruct((8, 128), jnp.float32),
        ),
        in_specs=[pl.BlockSpec(memory_space=pl.ANY)] * 4,
        out_specs=(
            pl.BlockSpec(memory_space=pltpu.VMEM),
            pl.BlockSpec(memory_space=pltpu.VMEM),
        ),
        scratch_shapes=[
            pltpu.VMEM((2, NY, 4, QUARTER, 128), BF),
            pltpu.VMEM((NX, 32, 1024), BF),
            pltpu.VMEM((4, NX, NZ, 2, 16, 1024), BF),
            pltpu.VMEM((2, NY, 3, QUARTER, 128), BF),
            pltpu.VMEM((2, NY, 2, QUARTER, 128), BF),
            pltpu.VMEM((2, NY, 1, QUARTER, 128), BF),
            pltpu.VMEM((4, QUARTER, COLS), jnp.float32),
            pltpu.VMEM((4, NX, QUARTER, COLS), BF),
            pltpu.VMEM((4, NX, QUARTER, COLS), BF),
            pltpu.VMEM((NZ, 4, 32, COLS), BF),
            pltpu.VMEM((NX, 1, COLS), jnp.float32),
            pltpu.VMEM((NZ, 1, COLS), jnp.float32),
            dma((2,)),
            dma((2,)),
            dma((2,)),
            dma((2,)),
            dma((2,)),
            dma((2,)),
            dma,
            dma,
            dma((4,)),
            dma((4,)),
            dma((3,)),
            dma((3, NX)),
            dma((4,)),
            dma((4, NX)),
            dma((3,)),
            dma((3,)),
            dma((3,)),
            dma((3,)),
            dma((3,)),
            dma((3,)),
            dma((4,)),
            dma((4,)),
            dma((4,)),
            dma((4,)),
            dma((2,)),
            dma((2,)),
        ],
        compiler_params=pltpu.CompilerParams(
            collective_id=0, has_side_effects=True, vmem_limit_bytes=40 * 1024 * 1024
        ),
        name="whiten",
    )(labeled, candidates, factor_rows, block_inverse)
    return whitened, explained.reshape(1024)


def solution(mesh):
    in_specs = (
        P(None, "row", "grp"),
        P(("grp", "row"), None),
        P(None, "row", None),
        P(None, "row", None),
    )
    out_specs = (P(None, "row", "grp"), P("grp"))
    return jax.shard_map(
        on_device, mesh=mesh, in_specs=in_specs, out_specs=out_specs, check_vma=False
    )
```

time: 800 us -> 86.5 us (0.11)
  the two profiles are of different devices: /device:TPU:8 before, /device:TPU:1 now
where the time goes in v1:
time: 86.5 us; the launch traced here: 85.8 us
  Pallas kernels  80.1 us (93%)
  local copies, waits for them, and re-layouts  5.06 us (6%)
    pallas_call x1, Pallas kernels, on_device(): pl.pallas_call(functools.partial(kernel, scale), out_shape=(jax.ShapeDtyp...  80.1 us
    unnamed x10, local copies, waits for them, and re-layouts  5.06 us

profile of v1, /device:TPU:1, one launch (start us, length us, event | category | flops | bytes accessed | tf_op | source)
XLA Modules:
  0.0 85.8 jit_solution(11982986693870960940)
XLA Ops:
  0.6 0.0 copy-start
  0.6 1.2 %copy-done = bf16[4,32,4096]{2,1,0:T(8,128)(2,1)S(1)} copy-done((bf16[4,32,4096]{2,1,0:T(8,128)(2,1)S(1)}, bf16[4,32,4096]{2,1,0:T(8,128)(2,1)}, u32[]{:S(2)}) %copy-start) | copy-done | bytes 1048600
  1.9 0.0 copy-start.1
  1.9 0.9 %copy-done.1 = bf16[4,32,1024]{2,1,0:T(8,128)(2,1)S(1)} copy-done((bf16[4,32,1024]{2,1,0:T(8,128)(2,1)S(1)}, bf16[4,32,1024]{2,1,0:T(8,128)(2,1)}, u32[]{:S(2)}) %copy-start.1) | copy-done | bytes 262168
  2.8 0.0 copy-start.2
  2.8 0.8 copy-done.2
  3.6 0.0 copy-start.3
  3.6 0.8 copy-done.3
  4.4 80.1 %whiten.1 = (bf16[4,32,1024]{2,1,0:T(8,128)(2,1)S(1)}, f32[8,128]{1,0:T(8,128)S(1)}) custom-call(bf16[4,32,128]{2,1,0:T(8,128)(2,1)S(1)} %copy-done.3, bf16[32,1024]{1,0:T(8,128)(2,1)S(1)} %copy-done.2, bf16[4,32,4096]{2,1,0:T(8,128)(2,1)S(1)} %copy-done, bf16[4,32,1024]{2,1,0:T(8,128)(2,1)S(1)} %copy-done.1), custom_call_target="tpu_custom_call" | custom-call | tf_op jit(solution)/shard_map/whiten/pallas_call | solution.py:403
  84.5 0.7 copy.8
  85.2 0.6 copy.9
Async XLA Ops:
  0.6 1.2 %copy-start = (bf16[4,32,4096]{2,1,0:T(8,128)(2,1)S(1)}, bf16[4,32,4096]{2,1,0:T(8,128)(2,1)}, u32[]{:S(2)}) copy-start(bf16[4,32,4096]{2,1,0:T(8,128)(2,1)} %fac.1) | copy-start | bytes 3145732
  1.9 0.9 %copy-start.1 = (bf16[4,32,1024]{2,1,0:T(8,128)(2,1)S(1)}, bf16[4,32,1024]{2,1,0:T(8,128)(2,1)}, u32[]{:S(2)}) copy-start(bf16[4,32,1024]{2,1,0:T(8,128)(2,1)} %inv.1) | copy-start | bytes 786436
  2.8 0.8 copy-start.2
  3.6 0.8 copy-start.3

commit v2 on v1

v2 whole, which is shorter than its diff:
```python
import functools
import math

import jax
import jax.numpy as jnp
from jax import lax
from jax.experimental import pallas as pl
from jax.experimental.pallas import tpu as pltpu
from jax.sharding import PartitionSpec as P

MESH = pl.DeviceIdType.MESH
BF = jnp.bfloat16
NX, NY, NZ = 4, 4, 8
QUARTER = 256
COLS = 128
VMEM_BYTES = 63 * 1024 * 1024
ITEMS = [("inv", 0), ("inv", 1), ("inv", 2), ("inv", 3)]
ITEMS += [("row", 0), ("row", 1), ("row", 2), ("row", 3)]
FULL = (True, False, False, False)
Y_STEPS = ((1, 3, 2), (1, 3, 2), (1, 3, 2), (1, 3, 2))
X_STEPS = ((1, 3, 2), (1, 3), (1, 3))


def dot(a, b):
    return jnp.dot(a, b, preferred_element_type=jnp.float32)


def kernel(
    scale,
    lab,
    cand,
    fac,
    inv,
    out,
    expl,
    mbuf0,
    mbuf1,
    mbuf2,
    mbuf3,
    cbuf,
    ibuf,
    kbuf,
    rbuf,
    wbuf,
    obuf,
    pick,
    epart,
    esum,
    own_sem,
    zs,
    zr,
    m1s,
    m1r,
    m2s,
    m2r,
    m3s,
    m3r,
    cs,
    cr,
    i2s,
    i2r,
    i3s,
    i3r,
    rs,
    rr,
    ws,
    wr,
    os,
    orr,
    es,
    er,
):
    g = lax.axis_index("grp")
    r = lax.axis_index("row")
    y, c = g // 2, g % 2
    x, z = r // NZ, r % NZ
    mbufs = (mbuf0, mbuf1, mbuf2, mbuf3)

    def x_peer(d):
        return (g, ((x + d) % NX) * NZ + z)

    def y_peer(d):
        return (((y + d) % NY) * 2 + c, r)

    def z_peer(d):
        return (g, x * NZ + (z + d) % NZ)

    core_peer = (y * 2 + 1 - c, r)

    def send(src, dst, ssem, rsem, device):
        pltpu.make_async_remote_copy(
            src_ref=src,
            dst_ref=dst,
            send_sem=ssem,
            recv_sem=rsem,
            device_id=device,
            device_id_type=MESH,
        ).start()

    def local(src, dst, sem):
        pltpu.make_async_copy(src, dst, sem).start()

    def await_bytes(ref, sem):
        pltpu.make_async_copy(ref, ref, sem).wait()

    def each_z(body):
        def step(d, carry):
            body(z_peer(d))
            return carry

        lax.fori_loop(1, NZ, step, 0)

    def rows_of(position):
        return pl.ds(pl.multiple_of(position * 32, 32), 32)

    own_rows = rows_of(z)

    side = 1 - 2 * c

    def along(distance):
        return (z + NZ + distance) % NZ

    def z_at(distance):
        return (g, x * NZ + along(distance))

    def slots(item, first, count):
        rows = pl.ds(pl.multiple_of(first * 32, 32), count * 32)
        return mbufs[item[1]].at[c, y, :, rows, :]

    def inv_slots(b, number, first, count):
        width = (number + 1) * QUARTER
        return ibuf.at[b, number, pl.ds(first, count), c, :, :width]

    def at_slots(item, body):
        if item[0] == "inv":
            by_x(lambda number: body(functools.partial(inv_slots, item[1], number)))
        else:
            body(functools.partial(slots, item))

    def by_x(body):
        for number in range(NX):
            pl.when(x == number)(functools.partial(body, number))

    def begin(item):
        n = ITEMS.index(item)

        def go(at):
            own = at(z, 1)
            await_bytes(own, own_sem.at[n])
            for distance in (2, -2, 1, -1):
                near = 0 if abs(distance) == 2 else 1
                send(own, own, zs.at[n], zr.at[n, near], z_at(distance))

        at_slots(item, go)

    def relay(item):
        n = ITEMS.index(item)

        def go(at):
            await_bytes(at(0, 2), zr.at[n, 0])
            for distance in (2, -2):
                one = at(along(-distance), 1)
                send(one, one, zs.at[n], zr.at[n, 2], z_at(distance // 2))
            far = at(along(-2 * side), 1)
            send(far, far, zs.at[n], zr.at[n, 2], z_at(2 * side))

        at_slots(item, go)

    def arrive(item):
        n = ITEMS.index(item)

        def go(at):
            await_bytes(at(0, 2), zr.at[n, 1])
            await_bytes(at(0, 3), zr.at[n, 2])

        at_slots(item, go)

    def row_first():
        own = slots(("row", 0), z, 1)
        await_bytes(own, own_sem.at[ITEMS.index(("row", 0))])
        each_z(lambda peer: send(own, own, m1s, m1r, peer))

    def row_y(b):
        block = mbufs[b].at[c, y]
        if b == 0:
            await_bytes(mbuf0.at[c, y, :, 0:224, :], m1r)
        else:
            arrive(("row", b))
        for d in Y_STEPS[b]:
            send(block, block, m2s.at[b], m2r.at[b, d], y_peer(d))

    def row_relay(b, step):
        lo = 0 if step == 1 else 128
        other = (y + NY - step) % NY
        await_bytes(mbufs[b].at[c, other], m2r.at[b, step])
        if len(Y_STEPS[b]) == 2:
            half = mbufs[b].at[c, other, :, lo : lo + 128, :]
            send(half, half, m2s.at[b], m2r.at[b, 2], y_peer(step))

    def row_core(b):
        await_bytes(mbufs[b].at[c, 0], m2r.at[b, 2])
        half = mbufs[b].at[c]
        send(half, half, m3s.at[b], m3r.at[b], core_peer)

    def row_wait(b):
        await_bytes(mbufs[b].at[1 - c], m3r.at[b])

    def inv_part(b, number, core, lo=0, hi=NZ):
        return ibuf.at[b, number, lo:hi, core, :, : (number + 1) * QUARTER]

    def inv_across(b, number):
        part = inv_part(b, number, c)
        send(part, part, i3s.at[b], i3r.at[b, number], core_peer)

    def inv_x(b):
        arrive(("inv", b))

        def go(number):
            part = inv_part(b, number, c)
            if FULL[b]:
                for d in X_STEPS[b]:
                    send(part, part, i2s.at[b], i2r.at[b, number], x_peer(d))
            inv_across(b, number)

        by_x(go)

    def inv_relay(b, step):
        lo = 0 if step == 1 else 4

        def go(number):
            other = (number + NX - step) % NX
            await_bytes(inv_part(b, other, c), i2r.at[b, other])
            if len(X_STEPS[b]) == 2:
                half = inv_part(b, other, c, lo, lo + 4)
                send(half, half, i2s.at[b], i2r.at[b, other], x_peer(step))
            inv_across(b, other)

        by_x(go)

    def inv_core(b):
        def go(number):
            far = (number + 2) % NX
            await_bytes(inv_part(b, far, c), i2r.at[b, far])
            inv_across(b, far)

        by_x(go)

    def inv_wait(b):
        if FULL[b]:
            for number in range(NX):
                await_bytes(inv_part(b, number, 1 - c), i3r.at[b, number])
        else:
            by_x(lambda number: await_bytes(inv_part(b, number, 1 - c), i3r.at[b, number]))

    def make_kernel(b):
        rows = jnp.concatenate([mbufs[b][k % 2, k // 2, 0] for k in range(8)], axis=1)
        sums = lax.dot_general(
            rows,
            cbuf[...].reshape(COLS, 1024),
            (((1,), (1,)), ((), ())),
            preferred_element_type=jnp.float32,
        )
        kbuf[b] = jnp.exp(sums * scale)

    def publish(b):
        rbuf[b, x] = kbuf[b].astype(BF)
        for d in range(1, NX):
            send(rbuf.at[b, x], rbuf.at[b, x], rs.at[b], rr.at[b], x_peer(d))

    def residual_wait(b):
        await_bytes(rbuf.at[b, 0:3], rr.at[b])

    def solve(b):
        residual = rbuf[b].reshape(1024, COLS)

        def rows(number):
            width = (number + 1) * QUARTER
            left = ibuf[b, number, :, :, :, :width].reshape(QUARTER, width)
            wbuf[b, number] = dot(left, residual[:width]).astype(BF)

        if FULL[b]:
            for number in range(NX):
                rows(number)
        else:
            by_x(rows)

    def share(b):
        for d in range(1, NX):
            send(wbuf.at[b, x], wbuf.at[b, x], ws.at[b], wr.at[b], x_peer(d))

    def share_wait(b):
        await_bytes(wbuf.at[b, 0:3], wr.at[b])

    def spread(b):
        dst = obuf.at[z, b]
        local(wbuf.at[b, x, own_rows, :], dst, orr.at[b])

        def step(d, carry):
            other = (z + d) % NZ
            send(
                wbuf.at[b, x, rows_of(other), :],
                dst,
                os.at[b],
                orr.at[b],
                (g, x * NZ + other),
            )
            return carry

        lax.fori_loop(1, NZ, step, 0)

    def update(j, b):
        parts = [mbufs[b][k % 2, k // 2, j + 1] for k in range(8)]
        panel = jnp.concatenate(parts, axis=1)
        kbuf[b] = kbuf[b] - dot(panel, wbuf[j].reshape(1024, COLS))

    def make_pickers():
        source = lax.broadcasted_iota(jnp.int32, (512, 128), 0)
        target = lax.broadcasted_iota(jnp.int32, (512, 128), 1)
        for chunk in range(NX):
            wanted = (target // 32) * 128 + chunk * 32 + target % 32
            pick[chunk] = jnp.where(source == wanted, 1.0, 0.0).astype(BF)

    def assemble(b):
        await_bytes(obuf.at[:, b], orr.at[b])
        for half in range(2):
            rows = jnp.concatenate([obuf[half * 4 + k, b] for k in range(4)], axis=1)
            for chunk in range(NX):
                at = (chunk * 2 + half) * 128
                out[b, :, at : at + 128] = dot(rows, pick[chunk]).astype(BF)

    barrier = pltpu.get_barrier_semaphore()
    peers = [x_peer(d) for d in range(1, NX)] + [y_peer(d) for d in range(1, NY)]
    peers += [z_peer(d) for d in range(1, NZ)] + [core_peer]
    for peer in peers:
        pl.semaphore_signal(barrier, inc=1, device_id=peer, device_id_type=MESH)
    def own_inv(b):
        def go(number):
            width = (number + 1) * QUARTER
            half = pl.ds(pl.multiple_of(c * 16, 16), 16)
            local(inv.at[b, half, :width], ibuf.at[b, number, z, c, :, :width], own_sem.at[b])

        by_x(go)

    def own_row(b):
        sem = own_sem.at[4 + b]
        local(lab.at[b], mbufs[b].at[c, y, 0, own_rows, :], sem)
        for j in range(b):
            cols = pl.ds(pl.multiple_of(j * 1024 + g * 128, 128), 128)
            local(fac.at[b, :, cols], mbufs[b].at[c, y, j + 1, own_rows, :], sem)

    own_row(0)
    local(cand, cbuf.at[x], own_sem.at[8])
    for b in range(4):
        own_inv(b)
        if b < 3:
            own_row(b + 1)
    pl.semaphore_wait(barrier, len(peers))

    i0, i1, i2, i3 = [("inv", b) for b in range(4)]
    m1, m2, m3 = [("row", b) for b in range(1, 4)]
    make_pickers()

    row_first()
    await_bytes(cbuf.at[x], own_sem.at[8])
    for d in range(1, NX):
        send(cbuf.at[x], cbuf.at[x], cs, cr, x_peer(d))
    begin(i0)
    begin(m1)
    begin(i1)
    relay(i0)
    relay(m1)
    row_y(0)
    begin(m2)
    inv_x(0)
    row_y(1)
    relay(i1)
    begin(i2)
    row_relay(0, 1)
    row_relay(0, 3)
    row_core(0)
    await_bytes(cbuf.at[0:3], cr)
    relay(m2)
    row_wait(0)
    make_kernel(0)
    publish(0)
    begin(m3)
    relay(i2)
    inv_x(1)
    begin(i3)
    row_relay(1, 1)
    row_relay(1, 3)
    row_core(1)
    row_y(2)
    inv_relay(0, 1)
    inv_relay(0, 3)
    inv_core(0)
    relay(m3)
    relay(i3)
    row_wait(1)
    make_kernel(1)
    inv_wait(0)
    residual_wait(0)
    solve(0)
    spread(0)
    update(0, 1)
    publish(1)
    inv_x(2)
    row_relay(2, 1)
    row_relay(2, 3)
    row_y(3)
    row_core(2)
    row_wait(2)
    make_kernel(2)
    update(0, 2)
    inv_wait(1)
    residual_wait(1)
    solve(1)
    share(1)
    spread(1)
    share_wait(1)
    update(1, 2)
    publish(2)
    row_relay(3, 1)
    row_relay(3, 3)
    inv_x(3)
    row_core(3)
    row_wait(3)
    make_kernel(3)
    update(0, 3)
    update(1, 3)
    inv_wait(2)
    residual_wait(2)
    solve(2)
    share(2)
    spread(2)
    share_wait(2)
    update(2, 3)
    publish(3)

    for b in range(3):
        assemble(b)
    await_bytes(mbuf0.at[c, y, :, 0:224, :], m1s)
    for b in range(4):
        if b > 0:
            await_bytes(mbufs[b].at[c, y, :, 0:224, :], zs.at[ITEMS.index(("row", b))])
        await_bytes(mbufs[b].at[c, 0:3], m2s.at[b])
        await_bytes(mbufs[b].at[c], m3s.at[b])
    await_bytes(cbuf.at[0:3], cs)
    def owed(number):
        for b in range(4):
            await_bytes(inv_part(b, number, c, 0, 7), zs.at[ITEMS.index(("inv", b))])
            if FULL[b]:
                for _ in X_STEPS[b]:
                    await_bytes(inv_part(b, number, c), i2s.at[b])
                if len(X_STEPS[b]) == 2:
                    await_bytes(inv_part(b, (number - 1) % NX, c, 0, 4), i2s.at[b])
                    await_bytes(inv_part(b, (number + 1) % NX, c, 4, 8), i2s.at[b])

    by_x(owed)
    for b in range(4):
        if FULL[b]:
            for number in range(NX):
                await_bytes(inv_part(b, number, c), i3s.at[b])
        else:
            by_x(lambda number: await_bytes(inv_part(b, number, c), i3s.at[b]))
            if b < 3:
                await_bytes(wbuf.at[b, 0:3], ws.at[b])
    inv_wait(3)
    residual_wait(3)
    solve(3)
    spread(3)

    total = jnp.zeros((1, COLS), jnp.float32)
    for b in range(4):
        values = wbuf[b, x].astype(jnp.float32)
        total = total + jnp.sum(values * values, axis=0, keepdims=True)
    epart[x] = total
    for d in range(1, NX):
        send(epart.at[x], epart.at[x], es.at[0], er.at[0], x_peer(d))
    await_bytes(epart.at[0:3], er.at[0])
    esum[z] = epart[0] + epart[1] + epart[2] + epart[3]
    each_z(lambda peer: send(esum.at[z], esum.at[z], es.at[1], er.at[1], peer))

    assemble(3)

    await_bytes(esum.at[0:7], er.at[1])
    lane = lax.broadcasted_iota(jnp.int32, (1, 128), 1) // 32
    for chunk in range(NX):
        for half in range(2):
            row = jnp.zeros((1, COLS), jnp.float32)
            for k in range(4):
                moved = pltpu.roll(esum[half * 4 + k], ((k - chunk) % 4) * 32, 1)
                row = jnp.where(lane == k, moved, row)
            expl[chunk * 2 + half : chunk * 2 + half + 1, :] = row

    for b in range(4):
        await_bytes(rbuf.at[b, 0:3], rs.at[b])
        await_bytes(obuf.at[0:7, b], os.at[b])
    await_bytes(epart.at[0:3], es.at[0])
    await_bytes(esum.at[0:7], es.at[1])


def on_device(labeled, candidates, factor_rows, block_inverse):
    dma = pltpu.SemaphoreType.DMA
    scale = 0.5 / math.sqrt(1024)
    whitened, explained = pl.pallas_call(
        functools.partial(kernel, scale),
        out_shape=(
            jax.ShapeDtypeStruct((4, 32, 1024), BF),
            jax.ShapeDtypeStruct((8, 128), jnp.float32),
        ),
        in_specs=[pl.BlockSpec(memory_space=pltpu.HBM)] * 4,
        out_specs=(
            pl.BlockSpec(memory_space=pltpu.VMEM),
            pl.BlockSpec(memory_space=pltpu.VMEM),
        ),
        scratch_shapes=[
            pltpu.VMEM((2, NY, 1, QUARTER, 128), BF),
            pltpu.VMEM((2, NY, 2, QUARTER, 128), BF),
            pltpu.VMEM((2, NY, 3, QUARTER, 128), BF),
            pltpu.VMEM((2, NY, 4, QUARTER, 128), BF),
            pltpu.VMEM((NX, 32, 1024), BF),
            pltpu.VMEM((4, NX, NZ, 2, 16, 1024), BF),
            pltpu.VMEM((4, QUARTER, COLS), jnp.float32),
            pltpu.VMEM((4, NX, QUARTER, COLS), BF),
            pltpu.VMEM((4, NX, QUARTER, COLS), BF),
            pltpu.VMEM((NZ, 4, 32, COLS), BF),
            pltpu.VMEM((NX, 512, 128), BF),
            pltpu.VMEM((NX, 1, COLS), jnp.float32),
            pltpu.VMEM((NZ, 1, COLS), jnp.float32),
            dma((9,)),
            dma((8,)),
            dma((8, 3)),
            dma,
            dma,
            dma((4,)),
            dma((4, NY)),
            dma((4,)),
            dma((4,)),
            dma,
            dma,
            dma((3,)),
            dma((3, NX)),
            dma((4,)),
            dma((4, NX)),
            dma((4,)),
            dma((4,)),
            dma((3,)),
            dma((3,)),
            dma((4,)),
            dma((4,)),
            dma((2,)),
            dma((2,)),
        ],
        compiler_params=pltpu.CompilerParams(
            collective_id=0, has_side_effects=True, vmem_limit_bytes=VMEM_BYTES
        ),
        name="whiten",
    )(labeled, candidates, factor_rows, block_inverse)
    return whitened, explained.reshape(1024)


def solution(mesh):
    in_specs = (
        P(None, "row", "grp"),
        P(("grp", "row"), None),
        P(None, "row", None),
        P(None, "row", None),
    )
    out_specs = (P(None, "row", "grp"), P("grp"))
    return jax.shard_map(
        on_device, mesh=mesh, in_specs=in_specs, out_specs=out_specs, check_vma=False
    )
```

time: 86.5 us -> 77.1 us (0.89)
  Pallas kernels: 80.1 us -> 73.6 us
  local copies, waits for them, and re-layouts: 5.06 us -> 2.27 us
    pallas_call x1, Pallas kernels: 80.1 us -> 73.6 us  [on_device(): pl.pallas_call(functools.partial(kernel, scale), out_shape=(jax.ShapeDtyp...]
    unnamed x10 -> x4, local copies, waits for them, and re-layouts: 5.06 us -> 2.27 us
where the time goes in v2:
time: 77.1 us; the launch traced here: 76.5 us
  Pallas kernels  73.6 us (95%)
  local copies, waits for them, and re-layouts  2.27 us (3%)
    pallas_call x1, Pallas kernels, on_device(): pl.pallas_call(functools.partial(kernel, scale), out_shape=(jax.ShapeDtyp...  73.6 us
    unnamed x4, local copies, waits for them, and re-layouts  2.27 us

profile of v2, /device:TPU:1, one launch (start us, length us, event | category | flops | bytes accessed | tf_op | source)
XLA Modules:
  0.0 76.5 jit_solution(6830114623861649630)
XLA Ops:
  0.6 73.6 %whiten.1 = (bf16[4,32,1024]{2,1,0:T(8,128)(2,1)}, f32[8,128]{1,0:T(8,128)}) custom-call(bf16[4,32,128]{2,1,0:T(8,128)(2,1)} %lab.1, bf16[32,1024]{1,0:T(8,128)(2,1)} %cand.1, bf16[4,32,4096]{2,1,0:T(8,128)(2,1)} %fac.1, bf16[4,32,1024]{2,1,0:T(8,128)(2,1)} %inv.1), custom_call_target="tpu_custom_call" | custom-call | tf_op jit(solution)/shard_map/whiten/pallas_call | solution.py:506
  74.2 0.0 copy-start
  74.3 1.7 %copy.8 = bf16[4,32,1024]{2,1,0:T(8,128)(2,1)} copy(bf16[4,32,1024]{2,1,0:T(8,128)(2,1)} %get-tuple-element.8) | data formatting | bytes 524288
  75.9 0.0 copy-done
  75.9 0.6 copy.9
Async XLA Ops:
  74.2 1.7 %copy-start = (f32[8,128]{1,0:T(8,128)S(1)}, f32[8,128]{1,0:T(8,128)}, u32[]{:S(2)}) copy-start(f32[8,128]{1,0:T(8,128)} %get-tuple-element.5) | copy-start | bytes 12292

commit v3 on v2

--- a/solution.py
+++ b/solution.py
@@ -16,9 +16,10 @@
 VMEM_BYTES = 63 * 1024 * 1024
 ITEMS = [("inv", 0), ("inv", 1), ("inv", 2), ("inv", 3)]
 ITEMS += [("row", 0), ("row", 1), ("row", 2), ("row", 3)]
+Z_DIRECT = ()
 FULL = (True, False, False, False)
 Y_STEPS = ((1, 3, 2), (1, 3, 2), (1, 3, 2), (1, 3, 2))
-X_STEPS = ((1, 3, 2), (1, 3), (1, 3))
+X_STEPS = ((1, 3), (1, 3), (1, 3))
 
 
 def dot(a, b):
@@ -45,7 +46,6 @@
     obuf,
     pick,
     epart,
-    esum,
     own_sem,
     zs,
     zr,
@@ -147,6 +147,9 @@
         def go(at):
             own = at(z, 1)
             await_bytes(own, own_sem.at[n])
+            if item in Z_DIRECT:
+                each_z(lambda peer: send(own, own, zs.at[n], zr.at[n, 0], peer))
+                return
             for distance in (2, -2, 1, -1):
                 near = 0 if abs(distance) == 2 else 1
                 send(own, own, zs.at[n], zr.at[n, near], z_at(distance))
@@ -155,6 +158,8 @@
 
     def relay(item):
         n = ITEMS.index(item)
+        if item in Z_DIRECT:
+            return
 
         def go(at):
             await_bytes(at(0, 2), zr.at[n, 0])
@@ -170,6 +175,9 @@
         n = ITEMS.index(item)
 
         def go(at):
+            if item in Z_DIRECT:
+                await_bytes(at(0, 7), zr.at[n, 0])
+                return
             await_bytes(at(0, 2), zr.at[n, 1])
             await_bytes(at(0, 3), zr.at[n, 2])
 
@@ -380,10 +388,10 @@
     row_core(0)
     await_bytes(cbuf.at[0:3], cr)
     relay(m2)
+    begin(m3)
     row_wait(0)
     make_kernel(0)
     publish(0)
-    begin(m3)
     relay(i2)
     inv_x(1)
     begin(i3)
@@ -465,25 +473,28 @@
             by_x(lambda number: await_bytes(inv_part(b, number, c), i3s.at[b]))
             if b < 3:
                 await_bytes(wbuf.at[b, 0:3], ws.at[b])
+    total = jnp.zeros((1, COLS), jnp.float32)
+    for b in range(3):
+        values = wbuf[b, x].astype(jnp.float32)
+        total = total + jnp.sum(values * values, axis=0, keepdims=True)
     inv_wait(3)
     residual_wait(3)
     solve(3)
     spread(3)
 
-    total = jnp.zeros((1, COLS), jnp.float32)
-    for b in range(4):
-        values = wbuf[b, x].astype(jnp.float32)
-        total = total + jnp.sum(values * values, axis=0, keepdims=True)
-    epart[x] = total
-    for d in range(1, NX):
-        send(epart.at[x], epart.at[x], es.at[0], er.at[0], x_peer(d))
-    await_bytes(epart.at[0:3], er.at[0])
-    esum[z] = epart[0] + epart[1] + epart[2] + epart[3]
-    each_z(lambda peer: send(esum.at[z], esum.at[z], es.at[1], er.at[1], peer))
-
+    tail = wbuf[3, x].astype(jnp.float32)
+    epart[r] = total + jnp.sum(tail * tail, axis=0, keepdims=True)
+
+    def tell(d, carry):
+        other = (r + d) % (NX * NZ)
+        send(epart.at[r], epart.at[r], es, er, (g, other))
+        return carry
+
+    lax.fori_loop(1, NX * NZ, tell, 0)
     assemble(3)
 
-    await_bytes(esum.at[0:7], er.at[1])
+    await_bytes(epart.at[0:31], er)
+    esum = [sum(epart[k + NZ * i] for i in range(1, NX)) + epart[k] for k in range(NZ)]
     lane = lax.broadcasted_iota(jnp.int32, (1, 128), 1) // 32
     for chunk in range(NX):
         for half in range(2):
@@ -496,8 +507,7 @@
     for b in range(4):
         await_bytes(rbuf.at[b, 0:3], rs.at[b])
         await_bytes(obuf.at[0:7, b], os.at[b])
-    await_bytes(epart.at[0:3], es.at[0])
-    await_bytes(esum.at[0:7], es.at[1])
+    await_bytes(epart.at[0:31], es)
 
 
 def on_device(labeled, candidates, factor_rows, block_inverse):
@@ -526,8 +536,7 @@
             pltpu.VMEM((4, NX, QUARTER, COLS), BF),
             pltpu.VMEM((NZ, 4, 32, COLS), BF),
             pltpu.VMEM((NX, 512, 128), BF),
-            pltpu.VMEM((NX, 1, COLS), jnp.float32),
-            pltpu.VMEM((NZ, 1, COLS), jnp.float32),
+            pltpu.VMEM((NX * NZ, 1, COLS), jnp.float32),
             dma((9,)),
             dma((8,)),
             dma((8, 3)),
@@ -549,8 +558,8 @@
             dma((3,)),
             dma((4,)),
             dma((4,)),
-            dma((2,)),
-            dma((2,)),
+            dma,
+            dma,
         ],
         compiler_params=pltpu.CompilerParams(
             collective_id=0, has_side_effects=True, vmem_limit_bytes=VMEM_BYTES

time: 77.1 us -> 75.5 us (0.979)
  Pallas kernels: 73.6 us -> 72.5 us
    pallas_call x1, Pallas kernels: 73.6 us -> 72.5 us  [on_device(): pl.pallas_call(functools.partial(kernel, scale), out_shape=(jax.ShapeDtyp...]
where the time goes in v3:
time: 75.5 us; the launch traced here: 75.4 us
  Pallas kernels  72.5 us (96%)
  local copies, waits for them, and re-layouts  2.27 us (3%)
    pallas_call x1, Pallas kernels, on_device(): pl.pallas_call(functools.partial(kernel, scale), out_shape=(jax.ShapeDtyp...  72.5 us
    unnamed x4, local copies, waits for them, and re-layouts  2.27 us

profile of v3, /device:TPU:1, one launch (start us, length us, event | category | flops | bytes accessed | tf_op | source)
XLA Modules:
  0.0 75.4 jit_solution(941591618868735557)
XLA Ops:
  0.6 72.5 %whiten.1 = (bf16[4,32,1024]{2,1,0:T(8,128)(2,1)}, f32[8,128]{1,0:T(8,128)}) custom-call(bf16[4,32,128]{2,1,0:T(8,128)(2,1)} %lab.1, bf16[32,1024]{1,0:T(8,128)(2,1)} %cand.1, bf16[4,32,4096]{2,1,0:T(8,128)(2,1)} %fac.1, bf16[4,32,1024]{2,1,0:T(8,128)(2,1)} %inv.1), custom_call_target="tpu_custom_call" | custom-call | tf_op jit(solution)/shard_map/whiten/pallas_call | solution.py:516
  73.1 0.0 copy-start
  73.2 1.7 %copy.8 = bf16[4,32,1024]{2,1,0:T(8,128)(2,1)} copy(bf16[4,32,1024]{2,1,0:T(8,128)(2,1)} %get-tuple-element.8) | data formatting | bytes 524288
  74.8 0.0 copy-done
  74.8 0.6 copy.9
Async XLA Ops:
  73.1 1.7 %copy-start = (f32[8,128]{1,0:T(8,128)S(1)}, f32[8,128]{1,0:T(8,128)}, u32[]{:S(2)}) copy-start(f32[8,128]{1,0:T(8,128)} %get-tuple-element.5) | copy-start | bytes 12292

commit v4 on v3

--- a/solution.py
+++ b/solution.py
@@ -272,19 +272,35 @@
 
     def publish(b):
         rbuf[b, x] = kbuf[b].astype(BF)
-        for d in range(1, NX):
-            send(rbuf.at[b, x], rbuf.at[b, x], rs.at[b], rr.at[b], x_peer(d))
+        own = rbuf.at[b, x]
+        if FULL[b]:
+            for d in range(1, NX):
+                send(own, own, rs.at[b], rr.at[b], x_peer(d))
+        else:
+
+            def below(number):
+                for other in range(NX - 1, number, -1):
+                    send(own, own, rs.at[b], rr.at[b], (g, other * NZ + z))
+
+            by_x(below)
 
     def residual_wait(b):
-        await_bytes(rbuf.at[b, 0:3], rr.at[b])
+        if FULL[b]:
+            await_bytes(rbuf.at[b, 0:3], rr.at[b])
+        else:
+
+            def above(number):
+                if number:
+                    await_bytes(rbuf.at[b, 0:number], rr.at[b])
+
+            by_x(above)
 
     def solve(b):
-        residual = rbuf[b].reshape(1024, COLS)
-
         def rows(number):
             width = (number + 1) * QUARTER
             left = ibuf[b, number, :, :, :, :width].reshape(QUARTER, width)
-            wbuf[b, number] = dot(left, residual[:width]).astype(BF)
+            residual = rbuf[b, : number + 1].reshape(width, COLS)
+            wbuf[b, number] = dot(left, residual).astype(BF)
 
         if FULL[b]:
             for number in range(NX):
@@ -505,7 +521,15 @@
             expl[chunk * 2 + half : chunk * 2 + half + 1, :] = row
 
     for b in range(4):
-        await_bytes(rbuf.at[b, 0:3], rs.at[b])
+        if FULL[b]:
+            await_bytes(rbuf.at[b, 0:3], rs.at[b])
+        else:
+
+            def sent(number):
+                if number < NX - 1:
+                    await_bytes(rbuf.at[b, 0 : NX - 1 - number], rs.at[b])
+
+            by_x(sent)
         await_bytes(obuf.at[0:7, b], os.at[b])
     await_bytes(epart.at[0:31], es)
 

time: 75.5 us -> 74.2 us (0.983)
  Pallas kernels: 72.5 us -> 71.2 us
    pallas_call x1, Pallas kernels: 72.5 us -> 71.2 us  [on_device(): pl.pallas_call(functools.partial(kernel, scale), out_shape=(jax.ShapeDtyp...]
where the time goes in v4:
time: 74.2 us; the launch traced here: 74.1 us
  Pallas kernels  71.2 us (96%)
  local copies, waits for them, and re-layouts  2.27 us (3%)
    pallas_call x1, Pallas kernels, on_device(): pl.pallas_call(functools.partial(kernel, scale), out_shape=(jax.ShapeDtyp...  71.2 us
    unnamed x4, local copies, waits for them, and re-layouts  2.27 us

profile of v4, /device:TPU:1, one launch (start us, length us, event | category | flops | bytes accessed | tf_op | source)
XLA Modules:
  0.0 74.1 jit_solution(4517027858214608682)
XLA Ops:
  0.6 71.2 %whiten.1 = (bf16[4,32,1024]{2,1,0:T(8,128)(2,1)}, f32[8,128]{1,0:T(8,128)}) custom-call(bf16[4,32,128]{2,1,0:T(8,128)(2,1)} %lab.1, bf16[32,1024]{1,0:T(8,128)(2,1)} %cand.1, bf16[4,32,4096]{2,1,0:T(8,128)(2,1)} %fac.1, bf16[4,32,1024]{2,1,0:T(8,128)(2,1)} %inv.1), custom_call_target="tpu_custom_call" | custom-call | tf_op jit(solution)/shard_map/whiten/pallas_call | solution.py:540
  71.8 0.0 copy-start
  71.8 1.7 %copy.8 = bf16[4,32,1024]{2,1,0:T(8,128)(2,1)} copy(bf16[4,32,1024]{2,1,0:T(8,128)(2,1)} %get-tuple-element.8) | data formatting | bytes 524288
  73.5 0.0 copy-done
  73.5 0.6 copy.9
Async XLA Ops:
  71.8 1.7 %copy-start = (f32[8,128]{1,0:T(8,128)S(1)}, f32[8,128]{1,0:T(8,128)}, u32[]{:S(2)}) copy-start(f32[8,128]{1,0:T(8,128)} %get-tuple-element.5) | copy-start | bytes 12292

commit v5 on v4

--- a/solution.py
+++ b/solution.py
@@ -496,7 +496,6 @@
     inv_wait(3)
     residual_wait(3)
     solve(3)
-    spread(3)
 
     tail = wbuf[3, x].astype(jnp.float32)
     epart[r] = total + jnp.sum(tail * tail, axis=0, keepdims=True)
@@ -507,6 +506,7 @@
         return carry
 
     lax.fori_loop(1, NX * NZ, tell, 0)
+    spread(3)
     assemble(3)
 
     await_bytes(epart.at[0:31], er)

time: 74.2 us -> 73.2 us (0.987)
  Pallas kernels: 71.2 us -> 70.2 us
    pallas_call x1, Pallas kernels: 71.2 us -> 70.2 us  [on_device(): pl.pallas_call(functools.partial(kernel, scale), out_shape=(jax.ShapeDtyp...]
where the time goes in v5:
time: 73.2 us; the launch traced here: 73.1 us
  Pallas kernels  70.2 us (96%)
  local copies, waits for them, and re-layouts  2.27 us (3%)
    pallas_call x1, Pallas kernels, on_device(): pl.pallas_call(functools.partial(kernel, scale), out_shape=(jax.ShapeDtyp...  70.2 us
    unnamed x4, local copies, waits for them, and re-layouts  2.27 us

profile of v5, /device:TPU:1, one launch (start us, length us, event | category | flops | bytes accessed | tf_op | source)
XLA Modules:
  0.0 73.1 jit_solution(9437978315812670196)
XLA Ops:
  0.6 70.2 %whiten.1 = (bf16[4,32,1024]{2,1,0:T(8,128)(2,1)}, f32[8,128]{1,0:T(8,128)}) custom-call(bf16[4,32,128]{2,1,0:T(8,128)(2,1)} %lab.1, bf16[32,1024]{1,0:T(8,128)(2,1)} %cand.1, bf16[4,32,4096]{2,1,0:T(8,128)(2,1)} %fac.1, bf16[4,32,1024]{2,1,0:T(8,128)(2,1)} %inv.1), custom_call_target="tpu_custom_call" | custom-call | tf_op jit(solution)/shard_map/whiten/pallas_call | solution.py:540
  70.9 0.0 copy-start
  70.9 1.7 %copy.8 = bf16[4,32,1024]{2,1,0:T(8,128)(2,1)} copy(bf16[4,32,1024]{2,1,0:T(8,128)(2,1)} %get-tuple-element.8) | data formatting | bytes 524288
  72.5 0.0 copy-done
  72.5 0.6 copy.9
Async XLA Ops:
  70.9 1.7 %copy-start = (f32[8,128]{1,0:T(8,128)S(1)}, f32[8,128]{1,0:T(8,128)}, u32[]{:S(2)}) copy-start(f32[8,128]{1,0:T(8,128)} %get-tuple-element.5) | copy-start | bytes 12292
